TPU v7x, 128 devices: a whole 4x4x4 slice. The times are simulated.
128 devices in a mesh: rows: 8 (over x_lo, z), lat: 16 (over y, x_hi, core).
Axes of the slice: x: 4 (x_hi: 2, x_lo: 2; x = x_hi * 2 + x_lo), y: 4, z: 4, core: 2. Of those that a mesh axis runs over, the one named last changes fastest.
Arguments:
- context: bfloat16 [768, 4096], P('rows', 'lat'), may hold values from -6 to 6
- out_weight: bfloat16 [4096, 4608], P('lat'), may hold values from -0.09375 to 0.09375
- residual: bfloat16 [768, 4608], P(('rows', 'lat')), may hold values from -6 to 6
- post_gain: float32 [4608], replicated, may hold values from 0.1 to 1.9
- enc_weight: bfloat16 [4608, 65536], P(None, ('rows', 'lat')), may hold values from -0.09375 to 0.09375
- enc_bias: float32 [65536], P(('rows', 'lat')), may hold values from -3 to 3
- thresholds: int32 [65536], P(('rows', 'lat')), may hold values from 2048 to 12287
- dec_weight: bfloat16 [65536, 4608], P(('rows', 'lat')), may hold values from -0.0234375 to 0.0234375
- dec_bias: float32 [4608], replicated, may hold values from -2 to 2
- first_moment: bfloat16 [65536, 4608], P(('rows', 'lat')), may hold values from -0.59765625 to 0.59765625
- second_moment: bfloat16 [65536, 4608], P(('rows', 'lat')), may hold values from 9.9658966e-05 to 0.0039978027
- pack_order: int32 [32], replicated, may hold values from 0 to 31, each once
- seq_lengths: int32 [8, 4], replicated, may hold values from 1 to 48, 96 in all within a row
Outputs:
- error: bfloat16 [768, 4608], P(('rows', 'lat'))
- adam_step: bfloat16 [65536, 4608], P(('rows', 'lat'))
Inputs may be any that keep to these rules, and one draw needn't show every extreme that they name: `pack_order`: slot k lies in pack k // 4; every sequence number appears once. seq_lengths[p, j] belongs to slot p * 4 + j; the lengths of each pack sum to 96.
All inputs are finite; a program needn't handle non-finite values.
Results may differ from a plain program's by a relative error of at most 0.0082.
Values may be sent and summed in bfloat16 or wider, within the bound.
A program may use at most 128 MiB of HBM per device.

v0:
```python
import math

import jax
import jax.numpy as jnp
from jax import lax
from jax.sharding import PartitionSpec as P

band_width = 0.25
beta_one = 0.9
beta_two = 0.999


def canonical_source(pack_order, seq_lengths, overall):
    lengths = seq_lengths.reshape(-1)
    slot_start = jnp.cumsum(lengths) - lengths
    seq_ids = jnp.arange(lengths.shape[0], dtype=jnp.int32)
    onehot = (pack_order[:, None] == seq_ids[None, :]).astype(jnp.int32)
    seq_length = jnp.sum(onehot * lengths[:, None], axis=0)
    seq_slot_start = jnp.sum(onehot * slot_start[:, None], axis=0)
    seq_start = jnp.cumsum(seq_length) - seq_length
    positions = jnp.arange(overall, dtype=jnp.int32)
    member = (positions[:, None] >= seq_start[None, :]).astype(jnp.int32)
    owner = jnp.sum(member, axis=1) - 1
    select = (owner[:, None] == seq_ids[None, :]).astype(jnp.int32)
    begin_canon = jnp.sum(select * seq_start[None, :], axis=1)
    begin_pack = jnp.sum(select * seq_slot_start[None, :], axis=1)
    return begin_pack + positions - begin_canon


def post_norm(attention, post_gain, residual):
    root_mean = jnp.sqrt(jnp.mean(attention * attention, axis=-1, keepdims=True) + 1e-06)
    return (residual.astype(jnp.float32) + post_gain * attention / root_mean).astype(jnp.bfloat16)


def body(
    context,
    out_weight,
    residual,
    post_gain,
    enc_weight,
    enc_bias,
    thresholds,
    dec_weight,
    dec_bias,
    first_moment,
    second_moment,
    pack_order,
    seq_lengths,
):
    own_count = residual.shape[0]
    head_terms = jnp.dot(context, out_weight, preferred_element_type=jnp.float32)
    attention_all = lax.psum(head_terms, "lat")
    attention = lax.dynamic_slice_in_dim(
        attention_all, lax.axis_index("lat") * own_count, own_count, 0
    )
    read = post_norm(attention, post_gain, residual)
    gathered = lax.all_gather(read, ("rows", "lat"), axis=0, tiled=True)
    overall = gathered.shape[0]
    source = canonical_source(pack_order, seq_lengths, overall)
    canonical = jnp.take(gathered, source, axis=0)
    preact = jnp.dot(canonical, enc_weight, preferred_element_type=jnp.float32) + enc_bias
    cutoff = thresholds.astype(jnp.float32) / 4096.0
    active = (preact * jnp.clip((preact - cutoff) / band_width + 0.5, 0.0, 1.0)).astype(
        jnp.bfloat16
    )
    device_rows = overall // lax.axis_size(("rows", "lat"))
    first_row = lax.axis_index(("rows", "lat")) * device_rows
    recon = lax.psum(
        jnp.dot(active, dec_weight, preferred_element_type=jnp.float32), ("rows", "lat")
    )
    error_all = (recon + dec_bias - canonical.astype(jnp.float32)).astype(jnp.bfloat16)
    error_out = lax.dynamic_slice_in_dim(error_all, first_row, device_rows, 0)
    gradient = lax.dot_general(
        active, error_all, (((0,), (0,)), ((), ())), preferred_element_type=jnp.float32
    ) / math.sqrt(overall)
    moment_one = beta_one * first_moment.astype(jnp.float32) + (1.0 - beta_one) * gradient
    moment_two = (
        beta_two * second_moment.astype(jnp.float32) + (1.0 - beta_two) * gradient * gradient
    )
    update = moment_one / (1.0 - beta_one**2) / (jnp.sqrt(moment_two / (1.0 - beta_two**2)) + 1e-08)
    return (error_out, update.astype(jnp.bfloat16))


def solution(mesh):
    return jax.shard_map(
        body,
        mesh=mesh,
        in_specs=(
            P("rows", "lat"),
            P("lat", None),
            P(("rows", "lat"), None),
            P(),
            P(None, ("rows", "lat")),
            P(("rows", "lat")),
            P(("rows", "lat")),
            P(("rows", "lat"), None),
            P(),
            P(("rows", "lat"), None),
            P(("rows", "lat"), None),
            P(),
            P(),
        ),
        out_specs=(P(("rows", "lat"), None), P(("rows", "lat"), None)),
        check_vma=False,
    )
```

profile of v0, /device:TPU:1, one launch (start us, length us, event | category | flops | bytes accessed | tf_op | source)
XLA Modules:
  0.0 615.3 jit_solution(287614027050953649)
XLA Ops:
  7.2 1.6 copy-done
  8.8 2.5 fusion.4
  11.4 146.6 %all-reduce.3.cloned.1.call-done = f32[96,4608]{1,0:T(8,128)} async-done(((f32[96,4608]{1,0:T(8,128)}), f32[96,4608]{1,0:T(8,128)}) %all-reduce.3.cloned.1.call-update) | async-done | bytes 1769488 | tf_op jit(solution)/shard_map/psum | solution.py:52
  158.0 1.1 multiply_reduce_fusion
  159.2 1.7 fusion.1
  161.0 0.8 copy.27
  161.7 0.1 mul.82
  161.8 0.1 reshape.129
  161.9 0.1 reduce.1
  162.1 0.7 select_reduce_fusion.2
  162.8 0.1 copy.28
  163.0 0.1 reduce
  163.1 0.1 convert_reduce_fusion
  163.2 0.1 select_reduce_fusion.1
  163.3 0.7 convert_multiply_fusion
  164.0 203.4 %all-gather.3.cloned.1.call-done = bf16[128,6,4608]{2,1,0:T(8,128)(2,1)} async-done(((bf16[1,6,4608]{2,1,0:T(8,128)(2,1)}), bf16[128,6,4608]{2,1,0:T(8,128)(2,1)}) %all-gather.3.cloned.1.call-update) | async-done | bytes 7077904 | tf_op jit(solution)/shard_map/all_gather | solution.py:57
  367.4 11.4 %reshape.128 = bf16[768,4608]{1,0:T(8,128)(2,1)} reshape(bf16[128,6,4608]{2,1,0:T(8,128)(2,1)} %all-gather.3.cloned.1.call-done) | data formatting | bytes 14155776
  378.8 17.3 %gather_fusion = bf16[768,4608]{1,0:T(8,128)(2,1)} fusion(bf16[768,4608]{1,0:T(8,128)(2,1)} %reshape.128, s32[1024]{0:T(1024)S(1)} %pad_clamp_fusion), kind=kCustom, calls=%fused_computation | custom fusion | bytes 14158848 | tf_op jit(solution)/shard_map/jit(_take)/gather | solution.py:60
  396.2 8.4 %multiply_convert_fusion = bf16[768,512]{1,0:T(8,128)(2,1)S(1)} fusion(bf16[4608,512]{1,0:T(8,128)(2,1)} %param.17, bf16[768,4608]{1,0:T(8,128)(2,1)} %gather_fusion, pred[768]{0:T(1024)(128)(4,1)S(1)} %compare_and_fusion, f32[512]{0:T(512)S(1)} %convert_multiply_fusion, f32[512]{0:T(512)S(1)} %copy-done.3), kind=kOutput, calls=%fused_computation.5 | convolution fusion | flops 3630170112 | bytes 12587776 | tf_op jit(solution)/shard_map/dot_general | solution.py:61
  404.6 9.5 %fusion.5 = f32[768,4608]{1,0:T(8,128)} fusion(bf16[768,512]{1,0:T(8,128)(2,1)S(1)} %multiply_convert_fusion, bf16[512,4608]{1,0:T(8,128)(2,1)} %param.20), kind=kOutput, calls=%fused_computation.28 | convolution fusion | flops 3623878656 | bytes 19660800 | tf_op jit(solution)/shard_map/dot_general | solution.py:69
  414.1 171.5 %all-reduce.5.cloned.1.call-done = f32[768,4608]{1,0:T(8,128)} async-done(((f32[768,4608]{1,0:T(8,128)}), f32[768,4608]{1,0:T(8,128)}) %all-reduce.5.cloned.1.call-update) | async-done | bytes 14155792 | tf_op jit(solution)/shard_map/psum | solution.py:68
  585.6 8.1 %subtract_convert_fusion = bf16[768,4608]{1,0:T(8,128)(2,1)S(1)} fusion(f32[768,4608]{1,0:T(8,128)} %all-reduce.5.cloned.1.call-done, f32[4608]{0:T(1024)S(1)} %copy-done.2, bf16[768,4608]{1,0:T(8,128)(2,1)} %gather_fusion, pred[768]{0:T(1024)(128)(4,1)S(1)} %compare_and_fusion), kind=kLoop, calls=%fused_computation.1 | loop fusion | flops 17694720 | bytes 28330752 | tf_op jit(solution)/shard_map/convert_element_type | solution.py:71
  593.8 0.7 constant_dynamic-slice_fusion
  594.4 14.3 %divide_convert_fusion = bf16[512,4608]{1,0:T(8,128)(2,1)} fusion(bf16[512,4608]{1,0:T(8,128)(2,1)} %param.23, bf16[512,4608]{1,0:T(8,128)(2,1)} %param.22, bf16[768,512]{1,0:T(8,128)(2,1)S(1)} %multiply_convert_fusion, bf16[768,4608]{1,0:T(8,128)(2,1)S(1)} %subtract_convert_fusion), kind=kOutput, calls=%fused_computation.2 | convolution fusion | flops 3659268096 | bytes 22020096 | tf_op jit(solution)/shard_map/dot_general | solution.py:73
  (22 shorter events, 0.4 us)
Async XLA Ops:
  7.2 1.7 copy-start
  7.2 150.9 %all-reduce.3.cloned.1.call-start = ((), (), s32[]{:S(2)}) async-start(), calls=%async_computation | async-start | bytes 3538944 | tf_op jit(solution)/shard_map/psum | solution.py:52
  11.4 356.0 %all-gather.3.cloned.1.call-start = ((), (), s32[]{:S(2)}) async-start(), calls=%async_computation.2 | async-start | bytes 9510912 | tf_op jit(solution)/shard_map/all_gather | solution.py:57
  160.9 424.7 %all-reduce.5.cloned.1.call-start = ((), (), s32[]{:S(2)}) async-start(), calls=%async_computation.1 | async-start | bytes 28311552 | tf_op jit(solution)/shard_map/psum | solution.py:68
  378.8 17.4 %copy-start.3 = (f32[512]{0:T(512)S(1)}, f32[512]{0:T(512)}, u32[]{:S(2)}) copy-start(f32[512]{0:T(512)} %param.18) | copy-start | bytes 6148
  414.1 171.5 %copy-start.2 = (f32[4608]{0:T(1024)S(1)}, f32[4608]{0:T(1024)}, u32[]{:S(2)}) copy-start(f32[4608]{0:T(1024)} %param.21) | copy-start | bytes 55300
  594.4 14.3 %copy-start.1 = (bf16[256,4608]{1,0:T(8,128)(2,1)S(1)}, bf16[256,4608]{1,0:T(8,128)(2,1)}, u32[]{:S(2)}) copy-start(bf16[256,4608]{1,0:T(8,128)(2,1)} %param.14) | copy-start | bytes 7077892
Sparse Core Ops, SparseCore 0:
  11.5 146.4 all-reduce.2
  161.0 206.3 all-gather.2
  414.2 171.3 all-reduce.4
where the time goes:
time: 616 us; the launch traced here: 615 us
  waiting for transfers between devices  521 us (85%)
  matrix products  34.7 us (6%)
  local copies, waits for them, and re-layouts  32.1 us (5%)
  between operations  13.8 us (2%)
  other arithmetic  13 us (2%)
    all_gather x1, waiting for transfers between devices, body(): gathered = lax.all_gather(read, ('rows', 'lat'), axis=0, tiled=True)  203 us
    psum x1, waiting for transfers between devices, body(): lax.psum(jnp.dot(active, dec_weight, preferred_element_type=jnp.float32),...  171 us
    psum x1, waiting for transfers between devices, body(): attention_all = lax.psum(head_terms, 'lat')  147 us
    gather x1, local copies, waits for them, and re-layouts, body(): canonical = jnp.take(gathered, source, axis=0)  17.3 us
    dot_general x1, matrix products, body(): lax.dot_general(active, error_all, (((0,), (0,)), ((), ())), preferred_el...  14.3 us
    unnamed x10, local copies, waits for them, and re-layouts  13.8 us
  transfers between devices with their start and end apart: 3, of which 3 were waited for; matrix products, arithmetic and copies ran while one was open for 0% of the time, Pallas kernels for 0%

commit v1 on v0

v1 whole, which is shorter than its diff:
```python
import math

import jax
import jax.numpy as jnp
from jax import lax
from jax.experimental import pallas as pl
from jax.experimental.pallas import tpu as pltpu
from jax.sharding import PartitionSpec as P

MESH = pl.DeviceIdType.MESH
F32 = jnp.float32
BF16 = jnp.bfloat16

D = 4608
TOKENS = 768
LOCAL = 512
QUART = 1152
SUB = 384
TILE = 16
THIRDS = range(3)
band_width = 0.25
beta_one = 0.9
beta_two = 0.999


def rem(a, b):
    return lax.rem(a, jnp.int32(b))


def tile_of(s, x, y, z):
    p = (x, y, z)
    i1, i2, i3 = p[s], p[(s + 1) % 3], p[(s + 2) % 3]
    return i1 // 2, i3, i2, i1 % 2


def columns_of(ref, t, y, s):
    return jnp.concatenate([ref[(s, t) + tile_of(s, x, y, z)] for x in range(4) for z in range(4)], axis=0)


def kernel(
    ctx, ow, res, gain, ebias, thr, dbias, porder, slens, enc_h, dec_h, m1_h, m2_h,
    err_o, adam_o,
    enc_v, dec_v, m1_v, m2_v, xb, pb, qb, eb, mb, fb, r2b, r1b,
    pa, sa, asum, sb, ar, rp, rr, stat, rb, act_t, gain_q, bias_q,
    load_sem, att_send, att_sib, att_recv, res_send, res_recv, stat_send, stat_recv,
    p1_send, p1_send0, p1_recv, ag_send, p2_recv, p3_recv, sib_recv,
    rs_send, q_recv, r3_recv, r2_recv, r1_recv, out_sem,
):
    r = lax.axis_index("rows")
    l = lax.axis_index("lat")
    c = rem(l, 2)
    xh = rem(l // 2, 2)
    y = l // 4
    xl = r // 4
    z = rem(r, 4)
    x = xh * 2 + xl
    own = c == xh
    me = (x, y, z)

    def device(x_, y_, z_, c_):
        return (rem(x_, 2) * 4 + z_, y_ * 4 + (x_ // 2) * 2 + c_)

    def ring(axis, d, core=None):
        p = [x, y, z]
        p[axis] = rem(p[axis] + d, 4)
        return device(*p, c if core is None else core)

    sibling = device(x, y, z, 1 - c)

    barrier = pltpu.get_barrier_semaphore()
    met = [(r, rem(l + d, 16)) for d in range(1, 16)]
    for core in range(2):
        met += [ring(0, 1, core), ring(0, 3, core)]
        met += [ring(2, d, core) for d in (1, 2, 3)]
    for dev in met:
        pl.semaphore_signal(barrier, inc=1, device_id=dev, device_id_type=MESH)

    loads = []
    for i, (h, v) in enumerate(((enc_h, enc_v), (dec_h, dec_v), (m1_h, m1_v), (m2_h, m2_v))):
        cp = pltpu.make_async_copy(h, v, load_sem.at[i])
        cp.start()
        loads.append(cp)

    for q in range(4):
        part = jnp.dot(ctx[...], ow[:, q * QUART:(q + 1) * QUART], preferred_element_type=F32)
        pa[q] = part.reshape(2, 48, QUART)
        sa[q] = pa[q, 1 - c].astype(BF16)
    rp[...] = jnp.zeros_like(rp)
    for q in range(4):
        cols = slice(q * QUART, (q + 1) * QUART)
        rp[q, 0:6] = res[:, cols]
        gain_q[q] = gain[cols].reshape(1, QUART)
        bias_q[q] = dbias[cols].reshape(1, QUART)

    def pick_rows():
        n = lax.broadcasted_iota(jnp.int32, (3, 256), 1)
        t = lax.broadcasted_iota(jnp.int32, (3, 256), 0)
        nx, nz, nr = n // 64, rem(n // 16, 4), rem(n, 16)
        token = (rem(nx, 2) * 4 + nz) * 96 + (nx // 2) * 48 + t * 16 + nr

        base = order = jnp.zeros((3, 256), jnp.int32)
        begin = jnp.int32(0)
        for k in range(32):
            end = begin + slens[k // 4, k % 4]
            inside = jnp.logical_and(token >= begin, token < end)
            base = jnp.where(inside, begin, base)
            order = jnp.where(inside, porder[k], order)
            begin = end
        place = token - base
        for k in range(32):
            place = place + jnp.where(porder[k] < order, slens[k // 4, k % 4], 0)
        first = (r * 16 + l) * 6
        for t in THIRDS:
            want = lax.broadcasted_iota(jnp.int32, (TILE, 256), 0) + first
            hit = jnp.logical_and(place[t:t + 1] == want, want < first + 6)
            act_t[t, LOCAL:LOCAL + TILE] = hit.astype(F32).astype(BF16)

    pick_rows()
    pl.semaphore_wait(barrier, len(met))

    def remote(src, dst, send, recv, dev):
        return pltpu.make_async_remote_copy(
            src_ref=src, dst_ref=dst, send_sem=send, recv_sem=recv, device_id=dev, device_id_type=MESH
        )

    def arrived(dst, sem):
        pltpu.make_async_copy(dst, dst, sem).wait()

    for d in (2, 1, 3, 0):
        q = rem(y + d, 4)
        remote(sa.at[q], asum.at[q], att_send.at[0], att_sib.at[q], sibling).start()
    rx = y // 2
    rslot = rem(y, 2) * 4 + xh * 2 + c
    stays = jnp.logical_and(rx == xh, c == rx)
    for d in (1, 2, 3):
        yd = rem(y + d, 4)
        remote(rp.at[yd], rr.at[rslot], res_send.at[0], res_recv.at[rslot], device(rx * 2 + xl, yd, z, rx)).start()

    @pl.when(stays)
    def _():
        pltpu.make_async_copy(rp.at[y], rr.at[rslot], res_recv.at[rslot]).start()

    @pl.when(jnp.logical_not(stays))
    def _():
        remote(rp.at[y], rr.at[rslot], res_send.at[1], res_recv.at[rslot], device(rx * 2 + xl, y, z, rx)).start()

    aslot = xh * 4 + y
    for d in (2, 1, 3, 0):
        yd = rem(y + d, 4)
        arrived(asum.at[yd], att_sib.at[yd])
        sb[yd] = (pa[yd, c] + asum[yd].astype(F32)).astype(BF16)
        if d:
            remote(sb.at[yd], ar.at[aslot], att_send.at[1], att_recv.at[aslot], device(c * 2 + xl, yd, z, c)).start()
        else:
            @pl.when(own)
            def _():
                pltpu.make_async_copy(sb.at[y], ar.at[aslot], att_recv.at[aslot]).start()

            @pl.when(jnp.logical_not(own))
            def _():
                remote(sb.at[y], ar.at[aslot], att_send.at[2], att_recv.at[aslot], device(c * 2 + xl, y, z, c)).start()

    def places(s):
        return me[s], me[(s + 1) % 3], me[(s + 2) % 3]

    def phase1(t):
        for s in THIRDS:
            i1, i2, i3 = places(s)
            k, j = i1 // 2, rem(i1, 2)
            src = rb.at[t, s]
            dst = xb.at[s, t, k, i3, i2, j]
            for d in (2, 1, 3):
                remote(src, dst, p1_send.at[0], p1_recv.at[t, s, j], ring(s, d, k)).start()

            @pl.when(k == c)
            def _():
                pltpu.make_async_copy(src, dst, p1_recv.at[t, s, j]).start()

            @pl.when(k != c)
            def _():
                remote(src, dst, p1_send0.at[s], p1_recv.at[t, s, j], sibling).start()

    def phase2(buf, w, t, s):
        i1, i2, i3 = places(s)
        piece = buf.at[s, t, c, i3, i2]
        for d in (2, 1, 3):
            remote(piece, piece, ag_send.at[w, 0], p2_recv.at[w, t, s, d], ring((s + 1) % 3, d)).start()

    def start_gather(t):
        for s in THIRDS:
            i1, i2, i3 = places(s)
            for j in range(2):
                arrived(xb.at[s, t, c, i3, i2, j], p1_recv.at[t, s, j])
            phase2(xb, 0, t, s)

    def phase3(buf, w, t):
        for s in THIRDS:
            i1, i2, i3 = places(s)
            for d in (1, 3, 2):
                arrived(buf.at[s, t, c, i3, rem(i2 + 4 - d, 4)], p2_recv.at[w, t, s, d])
            a3 = (s + 2) % 3
            half = [buf.at[s, t, c, i3, pl.ds(2 * h, 2)] for h in range(2)]
            for h in range(2):
                remote(half[h], half[h], ag_send.at[w, 1], p3_recv.at[w, t, s, 0, h], ring(a3, 1)).start()
                remote(half[1 - h], half[1 - h], ag_send.at[w, 1], p3_recv.at[w, t, s, 1, 1 - h], ring(a3, 3)).start()
        for s in THIRDS:
            share(buf, w, t, s, 0)

    def share(buf, w, t, s, d):
        part = buf.at[s, t, c, rem(places(s)[2] + d, 4)]
        remote(part, part, ag_send.at[w, 2], sib_recv.at[w, t, s, d], sibling).start()

    def forward(buf, w, t):
        for s in THIRDS:
            i3 = places(s)[2]
            a3 = (s + 2) % 3
            for side, d in ((0, 3), (1, 1)):
                piece = buf.at[s, t, c, rem(i3 + d, 4), pl.ds(2 * side, 2)]
                arrived(piece, p3_recv.at[w, t, s, side, side])
                remote(piece, piece, ag_send.at[w, 3], p3_recv.at[w, t, s, 2, side], ring(a3, 4 - d)).start()

    def finish_near(buf, w, t):
        for s in THIRDS:
            i3 = places(s)[2]
            for side, d in ((0, 3), (1, 1)):
                arrived(buf.at[s, t, c, rem(i3 + d, 4), pl.ds(2 - 2 * side, 2)], p3_recv.at[w, t, s, side, 1 - side])
                share(buf, w, t, s, d)

    def finish(buf, w, t):
        for s in THIRDS:
            i3 = places(s)[2]
            for side in range(2):
                arrived(buf.at[s, t, c, rem(i3 + 2, 4), pl.ds(2 * side, 2)], p3_recv.at[w, t, s, 2, side])
            share(buf, w, t, s, 2)

    def shared(buf, w, t):
        for s in THIRDS:
            i3 = places(s)[2]
            for d in range(4):
                arrived(buf.at[s, t, 1 - c, rem(i3 + d, 4)], sib_recv.at[w, t, s, d])

    def encode(t):
        rows = jnp.concatenate([columns_of(xb, t, q, s) for q in range(4) for s in THIRDS], axis=1)
        preact = jnp.dot(rows, enc_v[...], preferred_element_type=F32) + ebias[...]
        cutoff = thr[...].astype(F32) / 4096.0
        active = (preact * jnp.clip((preact - cutoff) / band_width + 0.5, 0.0, 1.0)).astype(BF16)
        act_t[t, 0:LOCAL] = active.T
        return active

    def decode(t, active):
        for q in range(4):
            part = jnp.dot(active, dec_v[:, q * QUART:(q + 1) * QUART], preferred_element_type=F32).astype(BF16)
            for s in THIRDS:
                for n in range(16):
                    pb[(s, t) + tile_of(s, n // 4, q, n % 4)] = part[n * TILE:(n + 1) * TILE, s * SUB:(s + 1) * SUB]
        for s in THIRDS:
            remote(pb.at[s, t, 1 - c], qb.at[s, t], rs_send.at[0], q_recv.at[t, s], sibling).start()

    def add_sibling(t, s, i3):
        return pb[s, t, c, i3].astype(F32) + qb[s, t, i3].astype(F32)

    def reduce_far(t):
        for s in THIRDS:
            i1, i2, i3 = places(s)
            a3 = (s + 2) % 3
            arrived(qb.at[s, t], q_recv.at[t, s])
            for d in (2, 1, 3):
                t3 = rem(i3 + d, 4)
                pb[s, t, c, t3] = add_sibling(t, s, t3).astype(BF16)
                for side in range(2):
                    src = pb.at[s, t, c, t3, pl.ds(2 * side, 2)]
                    if d == 2:
                        remote(src, mb.at[side, s, t], rs_send.at[1], r3_recv.at[t, s, 2, side], ring(a3, 1 + 2 * side)).start()
                    elif (d == 1) == (side == 1):
                        f = 0 if d == 1 else 1
                        remote(src, fb.at[f, s, t, pl.ds(2 * side, 2)], rs_send.at[2], r3_recv.at[t, s, f, side], ring(a3, d)).start()

    def reduce_near(t):
        for s in THIRDS:
            i1, i2, i3 = places(s)
            a3 = (s + 2) % 3
            for side, d in ((0, 1), (1, 3)):
                arrived(mb.at[side, s, t], r3_recv.at[t, s, 2, side])
                t3 = rem(i3 + d, 4)
                half = pl.ds(2 * side, 2)
                pb[s, t, c, t3, half] = (pb[s, t, c, t3, half].astype(F32) + mb[side, s, t].astype(F32)).astype(BF16)
                remote(pb.at[s, t, c, t3, half], fb.at[side, s, t, half], rs_send.at[2], r3_recv.at[t, s, side, side], ring(a3, d)).start()

    def reduce_mid(t):
        for s in THIRDS:
            i1, i2, i3 = places(s)
            total = add_sibling(t, s, i3)
            for f in range(2):
                for side in (1 - f, f):
                    arrived(fb.at[f, s, t, pl.ds(2 * side, 2)], r3_recv.at[t, s, f, side])
                total = total + fb[f, s, t].astype(F32)
            pb[s, t, c, i3] = total.astype(BF16)
            for d in (2, 1, 3):
                remote(pb.at[s, t, c, i3, rem(i2 + d, 4)], r2b.at[d - 1, s, t], rs_send.at[3], r2_recv.at[t, s, d],
                       ring((s + 1) % 3, d)).start()

    def reduce_last(t):
        for s in THIRDS:
            i1, i2, i3 = places(s)
            total = pb[s, t, c, i3, i2].astype(F32)
            for d in (1, 3, 2):
                arrived(r2b.at[d - 1, s, t], r2_recv.at[t, s, d])
                total = total + r2b[d - 1, s, t].astype(F32)
            r1b[s, t, i1] = total.astype(BF16)
            for d in (2, 1, 3):
                remote(r1b.at[s, t, i1], r1b.at[s, t, i1], rs_send.at[4], r1_recv.at[t, s, d], ring(s, d)).start()

    def make_error(t):
        for s in THIRDS:
            i1, i2, i3 = places(s)
            for d in (1, 3, 2):
                arrived(r1b.at[s, t, rem(i1 + 4 - d, 4)], r1_recv.at[t, s, d])
            for j in range(2):
                total = (r1b[s, t, 0, j].astype(F32) + r1b[s, t, 1, j].astype(F32)) + (
                    r1b[s, t, 2, j].astype(F32) + r1b[s, t, 3, j].astype(F32))
                bias = bias_q[2 * c + j if s == 1 else y, :, s * SUB:(s + 1) * SUB]
                canonical = xb[s, t, c, i3, i2, j].astype(F32)
                eb[s, t, c, i3, i2, j] = (total + bias - canonical).astype(BF16)
            phase2(eb, 1, t, s)

    @pl.when(own)
    def _():
        for i in range(8):
            arrived(ar.at[i], att_recv.at[i])
        att = ar[0].astype(F32)
        for i in range(1, 8):
            att = att + ar[i].astype(F32)
        stat[y] = jnp.broadcast_to(jnp.sum(att * att, axis=1, keepdims=True), (48, 128))
        for d in (2, 1, 3):
            remote(stat.at[y], stat.at[y], stat_send.at[0], stat_recv.at[y], ring(1, d)).start()
        for i in range(8):
            arrived(rr.at[i], res_recv.at[i])
        row = lax.broadcasted_iota(jnp.int32, (48, 128), 0)
        col = lax.broadcasted_iota(jnp.int32, (48, 128), 1)
        pick = (col == row + 10 * (row // 6)).astype(F32).astype(BF16)
        resid = jnp.dot(pick, rr[...].reshape(128, QUART), preferred_element_type=F32)
        scaled = gain_q[y] * att
        for d in (1, 3, 2):
            ys = rem(y + d, 4)
            arrived(stat.at[ys], stat_recv.at[ys])
        square = ((stat[0] + stat[1]) + (stat[2] + stat[3]))[:, 0:1]
        root_mean = jnp.sqrt(square / D + 1e-06)
        read = (resid + scaled / root_mean).astype(BF16)
        for t in THIRDS:
            for s in THIRDS:
                rb[t, s] = read[t * TILE:(t + 1) * TILE, s * SUB:(s + 1) * SUB]
            phase1(t)

    def update():
        loads[2].wait()
        loads[3].wait()
        one = 1.0 / (1.0 - beta_one**2)
        two = 1.0 / (1.0 - beta_two**2)
        copies = []
        for h in range(2):
            lo, hi = h * LOCAL // 2, (h + 1) * LOCAL // 2
            left = jnp.concatenate([act_t[t, lo:hi + h * TILE] for t in THIRDS], axis=1)
            for i in range(12):
                q, s = divmod(i, 3)
                cols = slice(q * QUART + s * SUB, q * QUART + (s + 1) * SUB)
                right = jnp.concatenate([columns_of(eb, t, q, s) for t in THIRDS], axis=0)
                grad = jnp.dot(left, right, preferred_element_type=F32)
                if h:
                    err_o[:, cols] = grad[hi - lo:hi - lo + 6].astype(BF16)
                g = grad[:hi - lo]
                first = (beta_one * one) * m1_v[lo:hi, cols].astype(F32) + ((1.0 - beta_one) * one / math.sqrt(TOKENS)) * g
                second = (beta_two * two) * m2_v[lo:hi, cols].astype(F32) + (((1.0 - beta_two) * two / TOKENS) * g) * g
                step = first * pltpu.reciprocal(second * lax.rsqrt(second) + 1e-08, approx=True)
                m1_v[lo:hi, cols] = step.astype(BF16)
            cp = pltpu.make_async_copy(m1_v.at[lo:hi], adam_o.at[lo:hi], out_sem.at[h])
            cp.start()
            copies.append(cp)
        for cp in copies:
            cp.wait()

    start_gather(0)
    start_gather(1)
    start_gather(2)
    phase3(xb, 0, 0)
    phase3(xb, 0, 1)
    forward(xb, 0, 0)
    phase3(xb, 0, 2)
    finish_near(xb, 0, 0)
    forward(xb, 0, 1)
    finish(xb, 0, 0)
    finish_near(xb, 0, 1)
    forward(xb, 0, 2)
    loads[0].wait()
    loads[1].wait()
    shared(xb, 0, 0)
    active = encode(0)
    finish(xb, 0, 1)
    finish_near(xb, 0, 2)
    decode(0, active)
    shared(xb, 0, 1)
    active = encode(1)
    finish(xb, 0, 2)
    reduce_far(0)
    decode(1, active)
    shared(xb, 0, 2)
    active = encode(2)
    reduce_near(0)
    reduce_far(1)
    decode(2, active)
    reduce_mid(0)
    reduce_near(1)
    reduce_far(2)
    reduce_last(0)
    reduce_mid(1)
    reduce_near(2)
    make_error(0)
    reduce_last(1)
    reduce_mid(2)
    phase3(eb, 1, 0)
    make_error(1)
    reduce_last(2)
    forward(eb, 1, 0)
    phase3(eb, 1, 1)
    make_error(2)
    finish_near(eb, 1, 0)
    forward(eb, 1, 1)
    phase3(eb, 1, 2)
    finish(eb, 1, 0)
    finish_near(eb, 1, 1)
    forward(eb, 1, 2)
    finish(eb, 1, 1)
    finish_near(eb, 1, 2)
    finish(eb, 1, 2)
    for t in THIRDS:
        shared(eb, 1, t)
    update()

    def sent(sem, n):
        for a in range(1, 4):
            for b in range(1, 4):
                for e in range(1, 5):
                    for f in range(1, 5):
                        if a * b * e * f * 2 == n:
                            view = xb.at[pl.ds(0, a), pl.ds(0, b), 0, pl.ds(0, e), pl.ds(0, f)]
                            pltpu.make_async_copy(view, view, sem).wait()
                            return
        if n % 64 == 0:
            view = xb.at[0, pl.ds(0, n // 64)]
        elif n % 9 == 0:
            view = xb.at[pl.ds(0, 3), pl.ds(0, 3), 0, pl.ds(0, n // 9), 0, 0]
        else:
            view = xb.at[0, pl.ds(0, n), 0, 0, 0, 0]
        assert math.prod(view.shape) == n * TILE * SUB
        pltpu.make_async_copy(view, view, sem).wait()

    sent(att_send.at[0], 36)
    sent(att_send.at[1], 27)
    sent(res_send.at[0], 9)

    @pl.when(jnp.logical_not(own))
    def _():
        sent(att_send.at[2], 9)

    @pl.when(jnp.logical_not(stays))
    def _():
        sent(res_send.at[1], 3)

    @pl.when(own)
    def _():
        pltpu.make_async_copy(stat.at[pl.ds(0, 3)], stat.at[pl.ds(0, 3)], stat_send.at[0]).wait()
        sent(p1_send.at[0], 27)
        for s in THIRDS:
            @pl.when(places(s)[0] // 2 != c)
            def _():
                sent(p1_send0.at[s], 3)

    for w in range(2):
        sent(ag_send.at[w, 0], 54)
        sent(ag_send.at[w, 1], 9 * 16)
        sent(ag_send.at[w, 2], 9 * 32)
        sent(ag_send.at[w, 3], 9 * 8)
    sent(rs_send.at[0], 9 * 32)
    sent(rs_send.at[1], 9 * 8)
    sent(rs_send.at[2], 9 * 16)
    sent(rs_send.at[3], 54)
    sent(rs_send.at[4], 54)


def body(context, out_weight, residual, post_gain, enc_weight, enc_bias, thresholds, dec_weight, dec_bias,
         first_moment, second_moment, pack_order, seq_lengths):
    vmem = pl.BlockSpec(memory_space=pltpu.VMEM)
    smem = pl.BlockSpec(memory_space=pltpu.SMEM)
    hbm = pl.BlockSpec(memory_space=pl.ANY)
    dma = pltpu.SemaphoreType.DMA

    def blocks(*dims):
        return pltpu.VMEM(dims + (TILE, SUB), BF16)

    scratch = [
        pltpu.VMEM((D, LOCAL), BF16), pltpu.VMEM((LOCAL, D), BF16),
        pltpu.VMEM((LOCAL, D), BF16), pltpu.VMEM((LOCAL, D), BF16),
        blocks(3, 3, 2, 4, 4, 2), blocks(3, 3, 2, 4, 4, 2), blocks(3, 3, 4, 4, 2), blocks(3, 3, 2, 4, 4, 2),
        blocks(2, 3, 3, 2, 2), blocks(2, 3, 3, 4, 2), blocks(3, 3, 3, 2), blocks(3, 3, 4, 2),
        pltpu.VMEM((4, 2, 48, QUART), F32), pltpu.VMEM((4, 48, QUART), BF16), pltpu.VMEM((4, 48, QUART), BF16),
        pltpu.VMEM((4, 48, QUART), BF16), pltpu.VMEM((8, 48, QUART), BF16),
        pltpu.VMEM((4, TILE, QUART), BF16), pltpu.VMEM((8, TILE, QUART), BF16),
        pltpu.VMEM((4, 48, 128), F32), blocks(3, 3),
        pltpu.VMEM((3, LOCAL + TILE, 16 * TILE), BF16),
        pltpu.VMEM((4, 1, QUART), F32), pltpu.VMEM((4, 1, QUART), F32),
        dma((4,)), dma((3,)), dma((4,)), dma((8,)), dma((2,)), dma((8,)), dma((1,)), dma((4,)),
        dma((1,)), dma((3,)), dma((3, 3, 2)), dma((2, 4)), dma((2, 3, 3, 4)), dma((2, 3, 3, 3, 2)), dma((2, 3, 3, 4)),
        dma((5,)), dma((3, 3)), dma((3, 3, 3, 2)), dma((3, 3, 4)), dma((3, 3, 4)), dma((12,)),
    ]
    return pl.pallas_call(
        kernel,
        out_shape=(jax.ShapeDtypeStruct((6, D), BF16), jax.ShapeDtypeStruct((LOCAL, D), BF16)),
        in_specs=[vmem] * 7 + [smem] * 2 + [hbm] * 4,
        out_specs=(vmem, hbm),
        scratch_shapes=scratch,
        compiler_params=pltpu.CompilerParams(
            collective_id=0, has_side_effects=True, vmem_limit_bytes=64 * 2**20
        ),
        cost_estimate=pl.CostEstimate(flops=11_100_000_000, bytes_accessed=31_000_000, transcendentals=0),
    )(
        context, out_weight, residual, post_gain, enc_bias.reshape(1, LOCAL),
        thresholds.reshape(1, LOCAL), dec_bias, pack_order, seq_lengths,
        enc_weight, dec_weight, first_moment, second_moment,
    )


def solution(mesh):
    return jax.shard_map(
        body,
        mesh=mesh,
        in_specs=(
            P("rows", "lat"), P("lat", None), P(("rows", "lat"), None), P(), P(None, ("rows", "lat")),
            P(("rows", "lat")), P(("rows", "lat")), P(("rows", "lat"), None), P(),
            P(("rows", "lat"), None), P(("rows", "lat"), None), P(), P(),
        ),
        out_specs=(P(("rows", "lat"), None), P(("rows", "lat"), None)),
        check_vma=False,
    )
```

time: 616 us -> 109 us (0.18)
  waiting for transfers between devices: 521 us -> 0 us
  Pallas kernels: 0 us -> 101 us
  matrix products: 34.7 us -> 0 us
  local copies, waits for them, and re-layouts: 32.1 us -> 7.7 us
  between operations: 13.8 us -> 0.64 us
  other arithmetic: 13 us -> 0 us
    psum x2 -> x0, waiting for transfers between devices: 318 us -> none  [the longest x1 171 us: body(): lax.psum(jnp.dot(active, dec_weight, preferred_element_type=jnp.float32),...]
    all_gather x1 -> x0, waiting for transfers between devices: 203 us -> none  [body(): gathered = lax.all_gather(read, ('rows', 'lat'), axis=0, tiled=True)]
    pallas_call x0 -> x1, Pallas kernels: none -> 101 us  [body(): pl.pallas_call(kernel, out_shape=(jax.ShapeDtypeStruct((6, D), BF16), jax...]
    dot_general x4 -> x0, matrix products: 34.7 us -> none  [the longest x1 14.3 us: body(): lax.dot_general(active, error_all, (((0,), (0,)), ((), ())), preferred_el...]
    gather x1 -> x0, local copies, waits for them, and re-layouts: 17.3 us -> none  [body(): canonical = jnp.take(gathered, source, axis=0)]
    convert_element_type x1 -> x0, other arithmetic: 8.14 us -> none  [body(): (recon + dec_bias - canonical.astype(jnp.float32)).astype(jnp.bfloat16)]
    unnamed x10 -> x3, local copies, waits for them, and re-layouts: 13.8 us -> 7.7 us
  transfers between devices with their start and end apart: 3 -> 0, of which waited for: 3 -> 0; matrix products, arithmetic and copies ran while one was open for 0% -> 0% of each run, Pallas kernels for 0% -> 0%
where the time goes in v1:
time: 109 us
  Pallas kernels  101 us (93%)
  local copies, waits for them, and re-layouts  7.7 us (7%)
    pallas_call x1, Pallas kernels, body(): pl.pallas_call(kernel, out_shape=(jax.ShapeDtypeStruct((6, D), BF16), jax...  101 us
    unnamed x3, local copies, waits for them, and re-layouts  7.7 us

profile of v1, /device:TPU:1, one launch (start us, length us, event | category | flops | bytes accessed | tf_op | source)
XLA Modules:
  0.0 109.3 jit_solution(2842748173001020471)
XLA Ops:
  0.6 1.3 %copy.15.slens = s32[8,4]{1,0:T(8,128)} copy(s32[8,4]{0,1:T(4,128)} %param.25) | data formatting | bytes 256 | tf_op args[12]
  2.0 100.9 %shard_map.140 = (bf16[6,4608]{1,0:T(8,128)(2,1)}, bf16[512,4608]{1,0:T(8,128)(2,1)}) custom-call(bf16[96,256]{1,0:T(8,128)(2,1)} %ctx.1, bf16[256,4608]{1,0:T(8,128)(2,1)} %ow.1, bf16[6,4608]{1,0:T(8,128)(2,1)} %res.1, f32[4608]{0:T(1024)} %gain.1, f32[1,512]{1,0:T(1,128)} %bitcast.2, s32[1,512]{1,0:T(1,128)} %bitcast.3, f32[4608]{0:T(1024)} %dbias.1, ...), custom_call_target="tpu_custom_call" | custom-call | flops 11100000256 | bytes 31000000 | tf_op jit(solution)/shard_map/pallas_call | solution.py:514
  102.9 1.5 %copy.18 = bf16[6,4608]{1,0:T(8,128)(2,1)} copy(bf16[6,4608]{1,0:T(8,128)(2,1)} %get-tuple-element.4) | data formatting | bytes 110592
  104.4 4.8 %copy.19 = bf16[512,4608]{1,0:T(8,128)(2,1)} copy(bf16[512,4608]{1,0:T(8,128)(2,1)} %get-tuple-element.5) | data formatting | bytes 9437184

commit v2 on v1

--- a/solution.py
+++ b/solution.py
@@ -41,7 +41,7 @@
     ctx, ow, res, gain, ebias, thr, dbias, porder, slens, enc_h, dec_h, m1_h, m2_h,
     err_o, adam_o,
     enc_v, dec_v, m1_v, m2_v, xb, pb, qb, eb, mb, fb, r2b, r1b,
-    pa, sa, asum, sb, ar, rp, rr, stat, rb, act_t, gain_q, bias_q,
+    pa, sa, asum, sb, ar, rp, rr, stat, rb, att_v, res_v, act_t, gain_q, bias_q,
     load_sem, att_send, att_sib, att_recv, res_send, res_recv, stat_send, stat_recv,
     p1_send, p1_send0, p1_recv, ag_send, p2_recv, p3_recv, sib_recv,
     rs_send, q_recv, r3_recv, r2_recv, r1_recv, out_sem,
@@ -74,12 +74,6 @@
         met += [ring(2, d, core) for d in (1, 2, 3)]
     for dev in met:
         pl.semaphore_signal(barrier, inc=1, device_id=dev, device_id_type=MESH)
-
-    loads = []
-    for i, (h, v) in enumerate(((enc_h, enc_v), (dec_h, dec_v), (m1_h, m1_v), (m2_h, m2_v))):
-        cp = pltpu.make_async_copy(h, v, load_sem.at[i])
-        cp.start()
-        loads.append(cp)
 
     for q in range(4):
         part = jnp.dot(ctx[...], ow[:, q * QUART:(q + 1) * QUART], preferred_element_type=F32)
@@ -115,7 +109,6 @@
             hit = jnp.logical_and(place[t:t + 1] == want, want < first + 6)
             act_t[t, LOCAL:LOCAL + TILE] = hit.astype(F32).astype(BF16)
 
-    pick_rows()
     pl.semaphore_wait(barrier, len(met))
 
     def remote(src, dst, send, recv, dev):
@@ -129,6 +122,28 @@
     for d in (2, 1, 3, 0):
         q = rem(y + d, 4)
         remote(sa.at[q], asum.at[q], att_send.at[0], att_sib.at[q], sibling).start()
+    aslot = xh * 4 + y
+
+    def exchange(t):
+        rows = slice(t * TILE, (t + 1) * TILE)
+        for d in (2, 1, 3, 0):
+            yd = rem(y + d, 4)
+            if t == 0:
+                arrived(asum.at[yd], att_sib.at[yd])
+            sb[t, yd] = (pa[yd, c, rows] + asum[yd, rows].astype(F32)).astype(BF16)
+            dst = ar.at[t, aslot]
+            if d:
+                remote(sb.at[t, yd], dst, att_send.at[1], att_recv.at[t, aslot], device(c * 2 + xl, yd, z, c)).start()
+            else:
+                @pl.when(own)
+                def _():
+                    pltpu.make_async_copy(sb.at[t, y], dst, att_recv.at[t, aslot]).start()
+
+                @pl.when(jnp.logical_not(own))
+                def _():
+                    remote(sb.at[t, y], dst, att_send.at[2], att_recv.at[t, aslot], device(c * 2 + xl, y, z, c)).start()
+
+    exchange(0)
     rx = y // 2
     rslot = rem(y, 2) * 4 + xh * 2 + c
     stays = jnp.logical_and(rx == xh, c == rx)
@@ -144,21 +159,8 @@
     def _():
         remote(rp.at[y], rr.at[rslot], res_send.at[1], res_recv.at[rslot], device(rx * 2 + xl, y, z, rx)).start()
 
-    aslot = xh * 4 + y
-    for d in (2, 1, 3, 0):
-        yd = rem(y + d, 4)
-        arrived(asum.at[yd], att_sib.at[yd])
-        sb[yd] = (pa[yd, c] + asum[yd].astype(F32)).astype(BF16)
-        if d:
-            remote(sb.at[yd], ar.at[aslot], att_send.at[1], att_recv.at[aslot], device(c * 2 + xl, yd, z, c)).start()
-        else:
-            @pl.when(own)
-            def _():
-                pltpu.make_async_copy(sb.at[y], ar.at[aslot], att_recv.at[aslot]).start()
-
-            @pl.when(jnp.logical_not(own))
-            def _():
-                remote(sb.at[y], ar.at[aslot], att_send.at[2], att_recv.at[aslot], device(c * 2 + xl, y, z, c)).start()
+    exchange(1)
+    exchange(2)
 
     def places(s):
         return me[s], me[(s + 1) % 3], me[(s + 2) % 3]
@@ -323,33 +325,45 @@
                 eb[s, t, c, i3, i2, j] = (total + bias - canonical).astype(BF16)
             phase2(eb, 1, t, s)
 
-    @pl.when(own)
-    def _():
+    def add_up(t):
         for i in range(8):
-            arrived(ar.at[i], att_recv.at[i])
-        att = ar[0].astype(F32)
+            arrived(ar.at[t, i], att_recv.at[t, i])
+        att = ar[t, 0].astype(F32)
         for i in range(1, 8):
-            att = att + ar[i].astype(F32)
-        stat[y] = jnp.broadcast_to(jnp.sum(att * att, axis=1, keepdims=True), (48, 128))
+            att = att + ar[t, i].astype(F32)
+        att_v[t] = att
+        stat[t, y] = jnp.broadcast_to(jnp.sum(att * att, axis=1, keepdims=True), (TILE, 128))
         for d in (2, 1, 3):
-            remote(stat.at[y], stat.at[y], stat_send.at[0], stat_recv.at[y], ring(1, d)).start()
+            remote(stat.at[t, y], stat.at[t, y], stat_send.at[0], stat_recv.at[t, y], ring(1, d)).start()
+
+    def place_residual():
         for i in range(8):
             arrived(rr.at[i], res_recv.at[i])
         row = lax.broadcasted_iota(jnp.int32, (48, 128), 0)
         col = lax.broadcasted_iota(jnp.int32, (48, 128), 1)
         pick = (col == row + 10 * (row // 6)).astype(F32).astype(BF16)
         resid = jnp.dot(pick, rr[...].reshape(128, QUART), preferred_element_type=F32)
-        scaled = gain_q[y] * att
+        res_v[...] = resid.reshape(3, TILE, QUART)
+
+    def normalise(t):
         for d in (1, 3, 2):
             ys = rem(y + d, 4)
-            arrived(stat.at[ys], stat_recv.at[ys])
-        square = ((stat[0] + stat[1]) + (stat[2] + stat[3]))[:, 0:1]
+            arrived(stat.at[t, ys], stat_recv.at[t, ys])
+        square = ((stat[t, 0] + stat[t, 1]) + (stat[t, 2] + stat[t, 3]))[:, 0:1]
         root_mean = jnp.sqrt(square / D + 1e-06)
-        read = (resid + scaled / root_mean).astype(BF16)
-        for t in THIRDS:
-            for s in THIRDS:
-                rb[t, s] = read[t * TILE:(t + 1) * TILE, s * SUB:(s + 1) * SUB]
-            phase1(t)
+        read = (res_v[t] + gain_q[y] * att_v[t] / root_mean).astype(BF16)
+        for s in THIRDS:
+            rb[t, s] = read[:, s * SUB:(s + 1) * SUB]
+        phase1(t)
+
+    @pl.when(own)
+    def _():
+        add_up(0)
+        place_residual()
+        add_up(1)
+        normalise(0)
+        add_up(2)
+        normalise(1)
 
     def update():
         loads[2].wait()
@@ -378,25 +392,38 @@
         for cp in copies:
             cp.wait()
 
+    def load(i, src, dst):
+        cp = pltpu.make_async_copy(src, dst, load_sem.at[i])
+        cp.start()
+        return cp
+
+    loads = [load(0, enc_h, enc_v), load(1, dec_h, dec_v)]
     start_gather(0)
+
+    @pl.when(own)
+    def _():
+        normalise(2)
+
     start_gather(1)
+    phase3(xb, 0, 0)
     start_gather(2)
-    phase3(xb, 0, 0)
     phase3(xb, 0, 1)
+    pick_rows()
+    loads += [load(2, m1_h, m1_v), load(3, m2_h, m2_v)]
     forward(xb, 0, 0)
     phase3(xb, 0, 2)
     finish_near(xb, 0, 0)
     forward(xb, 0, 1)
+    finish_near(xb, 0, 1)
     finish(xb, 0, 0)
-    finish_near(xb, 0, 1)
-    forward(xb, 0, 2)
     loads[0].wait()
     loads[1].wait()
     shared(xb, 0, 0)
     active = encode(0)
+    forward(xb, 0, 2)
+    decode(0, active)
     finish(xb, 0, 1)
     finish_near(xb, 0, 2)
-    decode(0, active)
     shared(xb, 0, 1)
     active = encode(1)
     finish(xb, 0, 2)
@@ -404,32 +431,32 @@
     decode(1, active)
     shared(xb, 0, 2)
     active = encode(2)
+    reduce_far(1)
     reduce_near(0)
-    reduce_far(1)
     decode(2, active)
-    reduce_mid(0)
     reduce_near(1)
     reduce_far(2)
+    reduce_mid(0)
+    reduce_near(2)
+    reduce_mid(1)
     reduce_last(0)
-    reduce_mid(1)
-    reduce_near(2)
+    reduce_mid(2)
+    reduce_last(1)
     make_error(0)
-    reduce_last(1)
-    reduce_mid(2)
+    reduce_last(2)
+    make_error(1)
+    make_error(2)
     phase3(eb, 1, 0)
-    make_error(1)
-    reduce_last(2)
+    phase3(eb, 1, 1)
+    phase3(eb, 1, 2)
     forward(eb, 1, 0)
-    phase3(eb, 1, 1)
-    make_error(2)
+    forward(eb, 1, 1)
+    forward(eb, 1, 2)
     finish_near(eb, 1, 0)
-    forward(eb, 1, 1)
-    phase3(eb, 1, 2)
+    finish_near(eb, 1, 1)
+    finish_near(eb, 1, 2)
     finish(eb, 1, 0)
-    finish_near(eb, 1, 1)
-    forward(eb, 1, 2)
     finish(eb, 1, 1)
-    finish_near(eb, 1, 2)
     finish(eb, 1, 2)
     for t in THIRDS:
         shared(eb, 1, t)
@@ -467,7 +494,7 @@
 
     @pl.when(own)
     def _():
-        pltpu.make_async_copy(stat.at[pl.ds(0, 3)], stat.at[pl.ds(0, 3)], stat_send.at[0]).wait()
+        pltpu.make_async_copy(stat.at[pl.ds(0, 3), pl.ds(0, 3)], stat.at[pl.ds(0, 3), pl.ds(0, 3)], stat_send.at[0]).wait()
         sent(p1_send.at[0], 27)
         for s in THIRDS:
             @pl.when(places(s)[0] // 2 != c)
@@ -502,12 +529,12 @@
         blocks(3, 3, 2, 4, 4, 2), blocks(3, 3, 2, 4, 4, 2), blocks(3, 3, 4, 4, 2), blocks(3, 3, 2, 4, 4, 2),
         blocks(2, 3, 3, 2, 2), blocks(2, 3, 3, 4, 2), blocks(3, 3, 3, 2), blocks(3, 3, 4, 2),
         pltpu.VMEM((4, 2, 48, QUART), F32), pltpu.VMEM((4, 48, QUART), BF16), pltpu.VMEM((4, 48, QUART), BF16),
-        pltpu.VMEM((4, 48, QUART), BF16), pltpu.VMEM((8, 48, QUART), BF16),
+        pltpu.VMEM((3, 4, TILE, QUART), BF16), pltpu.VMEM((3, 8, TILE, QUART), BF16),
         pltpu.VMEM((4, TILE, QUART), BF16), pltpu.VMEM((8, TILE, QUART), BF16),
-        pltpu.VMEM((4, 48, 128), F32), blocks(3, 3),
+        pltpu.VMEM((3, 4, TILE, 128), F32), blocks(3, 3), pltpu.VMEM((3, TILE, QUART), F32), pltpu.VMEM((3, TILE, QUART), F32),
         pltpu.VMEM((3, LOCAL + TILE, 16 * TILE), BF16),
         pltpu.VMEM((4, 1, QUART), F32), pltpu.VMEM((4, 1, QUART), F32),
-        dma((4,)), dma((3,)), dma((4,)), dma((8,)), dma((2,)), dma((8,)), dma((1,)), dma((4,)),
+        dma((4,)), dma((3,)), dma((4,)), dma((3, 8)), dma((2,)), dma((8,)), dma((1,)), dma((3, 4)),
         dma((1,)), dma((3,)), dma((3, 3, 2)), dma((2, 4)), dma((2, 3, 3, 4)), dma((2, 3, 3, 3, 2)), dma((2, 3, 3, 4)),
         dma((5,)), dma((3, 3)), dma((3, 3, 3, 2)), dma((3, 3, 4)), dma((3, 3, 4)), dma((12,)),
     ]

time: 109 us -> 109 us (level)
  no operation moved by 1% of the time
where the time goes in v2:
time: 109 us
  Pallas kernels  100 us (92%)
  local copies, waits for them, and re-layouts  7.7 us (7%)
    pallas_call x1, Pallas kernels, body(): pl.pallas_call(kernel, out_shape=(jax.ShapeDtypeStruct((6, D), BF16), jax...  100 us
    unnamed x3, local copies, waits for them, and re-layouts  7.7 us

profile of v2, /device:TPU:1, one launch (start us, length us, event | category | flops | bytes accessed | tf_op | source)
XLA Modules:
  0.0 108.8 jit_solution(124007975394528917)
XLA Ops:
  0.6 1.3 %copy.15.slens = s32[8,4]{1,0:T(8,128)} copy(s32[8,4]{0,1:T(4,128)} %param.25) | data formatting | bytes 256 | tf_op args[12]
  2.0 100.5 %shard_map.140 = (bf16[6,4608]{1,0:T(8,128)(2,1)}, bf16[512,4608]{1,0:T(8,128)(2,1)}) custom-call(bf16[96,256]{1,0:T(8,128)(2,1)} %ctx.1, bf16[256,4608]{1,0:T(8,128)(2,1)} %ow.1, bf16[6,4608]{1,0:T(8,128)(2,1)} %res.1, f32[4608]{0:T(1024)} %gain.1, f32[1,512]{1,0:T(1,128)} %bitcast.2, s32[1,512]{1,0:T(1,128)} %bitcast.3, f32[4608]{0:T(1024)} %dbias.1, ...), custom_call_target="tpu_custom_call" | custom-call | flops 11100000256 | bytes 31000000 | tf_op jit(solution)/shard_map/pallas_call | solution.py:541
  102.5 1.5 %copy.18 = bf16[6,4608]{1,0:T(8,128)(2,1)} copy(bf16[6,4608]{1,0:T(8,128)(2,1)} %get-tuple-element.4) | data formatting | bytes 110592
  104.0 4.8 %copy.19 = bf16[512,4608]{1,0:T(8,128)(2,1)} copy(bf16[512,4608]{1,0:T(8,128)(2,1)} %get-tuple-element.5) | data formatting | bytes 9437184
